TPU v7x, 32 devices: a whole 2x2x4 slice. The times are simulated.
32 devices in a mesh: groups: 2 (over x), depth: 8 (over z, y), lat: 2 (over core).
Axes of the slice: x: 2, y: 2, z: 4, core: 2. Of those that a mesh axis runs over, the one named last changes fastest.
Arguments:
- absorb: bfloat16 [64, 32, 4096], P('depth', ('groups', 'lat')), parts along dimension 1, may hold values from 0 to 0.35
- emission: bfloat16 [64, 32, 4096], P('depth', ('groups', 'lat')), parts along dimension 1, may hold values from 0.099609375 to 2
- measured: float32 [8, 32, 4096], P(None, ('groups', 'lat')), parts along dimension 1, may hold values from -6 to 6
- camera_view: int32 [8, 1], replicated, may hold values from 0 to 3
- offsets: int32 [4, 64], P(None, 'depth'), may hold values from -32 to 32
- fractions: float32 [4], replicated, may hold values from 0.2 to 0.8
Outputs:
- grad_absorb: float32 [64, 32, 4096], P('depth', ('groups', 'lat')), parts along dimension 1
- grad_emission: float32 [64, 32, 4096], P('depth', ('groups', 'lat')), parts along dimension 1
There are 2 independent parts, one for each index of `groups`. A program takes and returns all parts, laid end to end along the dimension named above; an argument that names none is the same for every part. Nothing has to cross between parts.
Inputs may be any that keep to these rules, and one draw needn't show every extreme that they name: `camera_view`: every view is seen by at least one camera.
All inputs are finite; a program needn't handle non-finite values.
Results may differ from a plain program's by a relative error of at most 0.0003.
Values may be sent and summed in bfloat16 or wider, within the bound.
A program may use at most 192 MiB of HBM per device.

v0:
```python
import functools

import jax
import jax.numpy as jnp
from jax import lax
from jax.experimental import pallas as pl
from jax.experimental.pallas import tpu as pltpu
from jax.sharding import PartitionSpec as P

reg_absorb = 20.0
reg_emit = 0.05
shift_max = 32
lanes = 128
vmem = pltpu.CompilerParams(vmem_limit_bytes=48 * 1024 * 1024)
MESH = pl.DeviceIdType.MESH


def tiles(value):
    return [value[:, i * lanes : (i + 1) * lanes] for i in range(value.shape[1] // lanes)]


def advance(parts, amount, lane):
    turned = [pltpu.roll(part, (lanes - amount) & (lanes - 1), axis=1) for part in parts]
    keep = lane < lanes - amount
    return [jnp.where(keep, turned[i], turned[i + 1]) for i in range(len(parts) - 1)]


def fill(field_ref, near_ref, step_ref, z):
    columns = field_ref.shape[2]
    field = field_ref[z].astype(jnp.float32)
    near = pltpu.roll(field, shift_max, axis=1)
    step = pltpu.roll(field, shift_max - 1, axis=1) - near
    near_ref[z, :, :columns] = near
    near_ref[z, :, columns:] = near[:, :lanes]
    step_ref[z, :, :columns] = step
    step_ref[z, :, columns:] = step[:, :lanes]


def sheared(near_ref, step_ref, z, start, width, amount, weight, lane):
    near = near_ref[z, :, pl.ds(start, width + lanes)]
    step = step_ref[z, :, pl.ds(start, width + lanes)]
    return advance(tiles(near + weight * step), amount, lane)


def first_kernel(
    absorb_ref, emit_ref, offs_ref, frac_ref, out_ref, edge_ref, near_a, step_a, near_e, step_e
):
    slices, rows, columns = absorb_ref.shape
    views = frac_ref.shape[0]
    count, piece = out_ref.shape[0], out_ref.shape[4]
    width = 1024
    lower = lax.axis_index("lat") == 0
    for z in range(slices):
        fill(absorb_ref, near_a, step_a, z)
        fill(emit_ref, near_e, step_e, z)
        for f, ref in enumerate((absorb_ref, emit_ref)):
            field = ref[z].astype(jnp.float32)
            edge_ref[f, z : z + 1, :] = jnp.where(lower, field[rows - 1 :], field[:1])
    lane = lax.broadcasted_iota(jnp.int32, (rows, lanes), 1)
    many = width // lanes

    def view_loop(v, _):
        weight = frac_ref[v]

        def chunk_loop(ch, _):
            start = pl.multiple_of(ch * width, width)
            run, light = None, None
            for z in range(slices):
                amount = offs_ref[v, z] + shift_max
                optical = sheared(near_a, step_a, z, start, width, amount, weight, lane)
                glowing = sheared(near_e, step_e, z, start, width, amount, weight, lane)
                trans = [jnp.exp(-o) for o in optical]
                radiance = [g * (1.0 - t) for g, t in zip(glowing, trans)]
                if z == 0:
                    run, light = trans, radiance
                else:
                    light = [l + r * x for l, r, x in zip(light, run, radiance)]
                    run = [r * t for r, t in zip(run, trans)]
            per = piece // lanes
            for i in range(many):
                dest = ch * (width // piece) + i // per
                cols = slice((i % per) * lanes, (i % per + 1) * lanes)
                out_ref[dest, v, 0, :, cols] = run[i]
                out_ref[dest, v, 1, :, cols] = light[i]
            return 0

        return lax.fori_loop(0, columns // width, chunk_loop, 0)

    lax.fori_loop(0, views, view_loop, 0)


def cross_kernel(
    mine_ref, measured_ref, cam_ref, edge_ref, back_ref, rim_ref, got, sent, s1, r1, s2, r2, s3, r3
):
    count, views, _, rows, piece = mine_ref.shape
    cameras = measured_ref.shape[0]
    me = lax.axis_index("depth")
    lat = lax.axis_index("lat")
    barrier = pltpu.get_barrier_semaphore()
    for p in range(1, count):
        pl.semaphore_signal(
            barrier, inc=1, device_id={"depth": lax.rem(me + p, count)}, device_id_type=MESH
        )
    pl.semaphore_signal(barrier, inc=1, device_id={"lat": 1 - lat}, device_id_type=MESH)
    pl.semaphore_wait(barrier, count)

    def out_copy(v, p):
        to = lax.rem(me + p, count)
        return pltpu.make_async_remote_copy(
            src_ref=mine_ref.at[to, v],
            dst_ref=got.at[me, v],
            send_sem=s1.at[v, p],
            recv_sem=r1.at[v, p],
            device_id={"depth": to},
            device_id_type=MESH,
        )

    def ret_copy(v, p):
        to = lax.rem(me + p, count)
        return pltpu.make_async_remote_copy(
            src_ref=sent.at[to, v],
            dst_ref=back_ref.at[me, v],
            send_sem=s2.at[v, p],
            recv_sem=r2.at[v, p],
            device_id={"depth": to},
            device_id_type=MESH,
        )

    for v in range(views):
        for p in range(1, count):
            out_copy(v, p).start()
    rim = pltpu.make_async_remote_copy(
        src_ref=edge_ref, dst_ref=rim_ref, send_sem=s3, recv_sem=r3,
        device_id={"lat": 1 - lat}, device_id_type=MESH,
    )
    rim.start()
    for v in range(views):
        got[me, v] = mine_ref[me, v]
    start = pl.multiple_of(me * piece, piece)
    for v in range(views):
        for p in range(1, count):
            out_copy(v, p).wait_recv()
        fronts = [jnp.ones((rows, piece), jnp.float32)]
        for j in range(count):
            fronts.append(fronts[-1] * got[j, v, 0])
        behind = jnp.zeros((rows, piece), jnp.float32)
        for j in reversed(range(count)):
            sent[j, v, 1] = behind
            behind = got[j, v, 1] + got[j, v, 0] * behind
        adjoint = jnp.zeros((rows, piece), jnp.float32)
        for k in range(cameras):
            seen = jnp.where(cam_ref[k, 0] == v, 1.0, 0.0).astype(jnp.float32)
            adjoint += seen * (behind - measured_ref[k, :, pl.ds(start, piece)])
        for j in range(count):
            sent[j, v, 0] = adjoint * fronts[j]
        for p in range(1, count):
            ret_copy(v, p).start()
        back_ref[me, v] = sent[me, v]
    rim.wait()
    for v in range(views):
        for p in range(1, count):
            out_copy(v, p).wait_send()
            ret_copy(v, p).wait()


def second_kernel(
    absorb_ref, emit_ref, offs_ref, frac_ref, back_ref, rim_ref, ga_ref, ge_ref,
    near_a, step_a, near_e, step_e, grad_a, grad_e, keep,
):
    slices, rows, columns = absorb_ref.shape
    views = frac_ref.shape[0]
    count, piece = back_ref.shape[0], back_ref.shape[4]
    width = min(512, columns)
    lower = lax.axis_index("lat") == 0
    for z in range(slices):
        fill(absorb_ref, near_a, step_a, z)
        fill(emit_ref, near_e, step_e, z)
    lane = lax.broadcasted_iota(jnp.int32, (rows, lanes), 1)
    many = width // lanes
    per = piece // lanes

    def view_loop(v, _):
        weight = frac_ref[v]

        def chunk_loop(ch, _):
            start = pl.multiple_of(ch * width, width)

            def entering(q):
                if piece >= width:
                    first = ch // (piece // width)
                    inner = pl.multiple_of((ch % (piece // width)) * width, width)
                    return tiles(back_ref[first, v, q, :, pl.ds(inner, width)])
                parts = []
                for i in range(many):
                    cols = slice((i % per) * lanes, (i % per + 1) * lanes)
                    parts.append(back_ref[ch * (width // piece) + i // per, v, q, :, cols])
                return parts

            run = entering(0)
            for z in range(slices):
                amount = offs_ref[v, z] + shift_max
                optical = sheared(near_a, step_a, z, start, width, amount, weight, lane)
                glowing = sheared(near_e, step_e, z, start, width, amount, weight, lane)
                for i in range(many):
                    trans = jnp.exp(-optical[i])
                    cols = slice(i * lanes, (i + 1) * lanes)
                    keep[z, 0, :, cols] = trans
                    keep[z, 1, :, cols] = glowing[i]
                    keep[z, 2, :, cols] = run[i]
                    run[i] = run[i] * trans
            behind = entering(1)
            for z in reversed(range(slices)):
                for i in range(many):
                    cols = slice(i * lanes, (i + 1) * lanes)
                    trans, glow, before = keep[z, 0, :, cols], keep[z, 1, :, cols], keep[z, 2, :, cols]
                    opaque = 1.0 - trans
                    at = pl.ds(pl.multiple_of(start + i * lanes, lanes), lanes)
                    grad_e[v, z, :, at] = before * opaque
                    grad_a[v, z, :, at] = before * trans * (glow - behind[i])
                    behind[i] = glow * opaque + trans * behind[i]
            return 0

        lax.fori_loop(0, columns // width, chunk_loop, 0)
        for z in range(slices):
            grad_a[v, z, :, columns:] = grad_a[v, z, :, :lanes]
            grad_e[v, z, :, columns:] = grad_e[v, z, :, :lanes]
        return 0

    lax.fori_loop(0, views, view_loop, 0)

    row = lax.broadcasted_iota(jnp.int32, (rows, columns), 0)
    col = lax.broadcasted_iota(jnp.int32, (rows, columns), 1)

    def slice_loop(z, _):
        for f, (field_ref, grad, out, reg) in enumerate(
            ((absorb_ref, grad_a, ga_ref, reg_absorb), (emit_ref, grad_e, ge_ref, reg_emit))
        ):
            near, far = [], []
            for ch in range(columns // width):
                total_near, total_far = None, None
                for v in range(views):
                    weight = frac_ref[v]
                    parts = tiles(grad[v, z, :, ch * width : (ch + 1) * width + lanes])
                    moved = advance(parts, shift_max - offs_ref[v, z], lane)
                    a = [(1.0 - weight) * m for m in moved]
                    b = [weight * m for m in moved]
                    total_near = a if v == 0 else [x + y for x, y in zip(total_near, a)]
                    total_far = b if v == 0 else [x + y for x, y in zip(total_far, b)]
                near += total_near
                far += total_far
            total = pltpu.roll(jnp.concatenate(near, axis=1), shift_max, axis=1)
            total += pltpu.roll(jnp.concatenate(far, axis=1), shift_max + 1, axis=1)
            field = field_ref[z].astype(jnp.float32)
            edge = rim_ref[f, pl.ds(z, 1), :]
            up = jnp.where(row == 0, jnp.where(lower, 0.0, edge), pltpu.roll(field, 1, axis=0))
            down = jnp.where(
                row == rows - 1, jnp.where(lower, edge, 0.0), pltpu.roll(field, rows - 1, axis=0)
            )
            left = jnp.where(col == 0, 0.0, pltpu.roll(field, 1, axis=1))
            right = jnp.where(col == columns - 1, 0.0, pltpu.roll(field, columns - 1, axis=1))
            out[z] = total - reg * (down + up + right + left - 4.0 * field)
        return 0

    lax.fori_loop(0, slices, slice_loop, 0)


def body(absorb, emission, measured, camera_view, offsets, fractions):
    slices, rows, columns = absorb.shape
    views = offsets.shape[0]
    count = lax.axis_size("depth")
    piece = columns // count
    whole = pl.BlockSpec(memory_space=pltpu.VMEM)
    scalar = pl.BlockSpec(memory_space=pltpu.SMEM)
    f32 = jnp.float32
    wide = pltpu.VMEM((slices, rows, columns + lanes), f32)
    blocks = (count, views, 2, rows, piece)
    sums, edge = pl.pallas_call(
        first_kernel,
        out_shape=(
            jax.ShapeDtypeStruct(blocks, f32),
            jax.ShapeDtypeStruct((2, slices, columns), f32),
        ),
        in_specs=[whole, whole, scalar, scalar],
        out_specs=(whole, whole),
        scratch_shapes=[wide] * 4,
        compiler_params=vmem,
        name="bricks",
    )(absorb, emission, offsets, fractions)
    dma = pltpu.SemaphoreType.DMA
    back, rim = pl.pallas_call(
        cross_kernel,
        out_shape=(
            jax.ShapeDtypeStruct(blocks, f32),
            jax.ShapeDtypeStruct((2, slices, columns), f32),
        ),
        in_specs=[whole, whole, scalar, whole],
        out_specs=(whole, whole),
        scratch_shapes=[
            pltpu.VMEM(blocks, f32),
            pltpu.VMEM(blocks, f32),
            dma((views, count)), dma((views, count)), dma((views, count)), dma((views, count)),
            dma, dma,
        ],
        compiler_params=pltpu.CompilerParams(
            vmem_limit_bytes=32 * 1024 * 1024, collective_id=0, has_side_effects=True
        ),
        name="exchange",
    )(sums, measured, camera_view, edge)
    grads = pltpu.VMEM((views, slices, rows, columns + lanes), f32)
    return pl.pallas_call(
        second_kernel,
        out_shape=(
            jax.ShapeDtypeStruct(absorb.shape, f32),
            jax.ShapeDtypeStruct(absorb.shape, f32),
        ),
        in_specs=[whole, whole, scalar, scalar, whole, whole],
        out_specs=(whole, whole),
        scratch_shapes=[wide] * 4 + [grads, grads, pltpu.VMEM((slices, 3, rows, 512), f32)],
        compiler_params=vmem,
        name="gradients",
    )(absorb, emission, offsets, fractions, back, rim)


def solution(mesh):
    placed = (
        P("depth", ("groups", "lat"), None),
        P("depth", ("groups", "lat"), None),
        P(None, ("groups", "lat"), None),
        P(),
        P(None, "depth"),
        P(),
    )
    return jax.shard_map(
        body,
        mesh=mesh,
        in_specs=placed,
        out_specs=(P("depth", ("groups", "lat"), None), P("depth", ("groups", "lat"), None)),
        check_vma=False,
    )
```

profile of v0, /device:TPU:0, one launch (start us, length us, event | category | flops | bytes accessed | tf_op | source)
XLA Modules:
  0.0 73.8 jit_solution(1980585016847354258)
XLA Ops:
  0.6 0.0 copy-start.4
  0.6 0.0 copy-start.3
  0.7 0.7 %copy.8.cam_ref = s32[8,1]{1,0:T(8,128)S(1)} copy(s32[8,1]{0,1:T(1,128)} %param.9) | data formatting | bytes 64 | tf_op args[3]
  1.4 0.0 copy-done.4
  1.4 0.0 copy-done.3
  1.4 0.0 copy-start
  1.4 1.0 %copy-done = bf16[8,8,4096]{2,1,0:T(8,128)(2,1)S(1)} copy-done((bf16[8,8,4096]{2,1,0:T(8,128)(2,1)S(1)}, bf16[8,8,4096]{2,1,0:T(8,128)(2,1)}, u32[]{:S(2)}) %copy-start) | copy-done | bytes 524312
  2.4 0.0 copy-start.1
  2.4 1.0 %copy-done.1 = bf16[8,8,4096]{2,1,0:T(8,128)(2,1)S(1)} copy-done((bf16[8,8,4096]{2,1,0:T(8,128)(2,1)S(1)}, bf16[8,8,4096]{2,1,0:T(8,128)(2,1)}, u32[]{:S(2)}) %copy-start.1) | copy-done | bytes 524312
  3.5 0.0 copy-start.2
  3.5 5.1 %bricks.1 = (f32[8,4,2,8,512]{4,3,2,1,0:T(8,128)S(1)}, f32[2,8,4096]{2,1,0:T(8,128)S(1)}) custom-call(bf16[8,8,4096]{2,1,0:T(8,128)(2,1)S(1)} %copy-done, bf16[8,8,4096]{2,1,0:T(8,128)(2,1)S(1)} %copy-done.1, s32[4,8]{1,0:T(4,128)S(1)} %copy-done.3, f32[4]{0:T(128)S(1)} %copy-done.4), custom_call_target="tpu_custom_call" | custom-call | tf_op jit(solution)/shard_map/bricks/pallas_call | solution.py:277
  8.6 0.0 copy-done.2
  8.6 52.3 %exchange.1 = (f32[8,4,2,8,512]{4,3,2,1,0:T(8,128)S(1)}, f32[2,8,4096]{2,1,0:T(8,128)S(1)}) custom-call(f32[8,4,2,8,512]{4,3,2,1,0:T(8,128)S(1)} %get-tuple-element.6.mine_ref, f32[8,8,4096]{2,1,0:T(8,128)S(1)} %copy-done.2, s32[8,1]{1,0:T(8,128)S(1)} %copy.8.cam_ref, f32[2,8,4096]{2,1,0:T(8,128)S(1)} %get-tuple-element.7.edge_ref), custom_call_target="tpu_custom_call" | custom-call | tf_op jit(solution)/shard_map/exchange/pallas_call | solution.py:290
  60.9 12.9 %gradients.1 = (f32[8,8,4096]{2,1,0:T(8,128)}, f32[8,8,4096]{2,1,0:T(8,128)}) custom-call(bf16[8,8,4096]{2,1,0:T(8,128)(2,1)S(1)} %copy-done, bf16[8,8,4096]{2,1,0:T(8,128)(2,1)S(1)} %copy-done.1, s32[4,8]{1,0:T(4,128)S(1)} %copy-done.3, f32[4]{0:T(128)S(1)} %copy-done.4, f32[8,4,2,8,512]{4,3,2,1,0:T(8,128)S(1)} %get-tuple-element.8.back_ref, ...), custom_call_target="tpu_custom_call" | custom-call | tf_op jit(solution)/shard_map/gradients/pallas_call | solution.py:310
Async XLA Ops:
  0.6 0.8 %copy-start.4 = (f32[4]{0:T(128)S(1)}, f32[4]{0:T(128)}, u32[]{:S(2)}) copy-start(f32[4]{0:T(128)} %frac_ref.3) | copy-start | bytes 52
  0.6 0.8 %copy-start.3 = (s32[4,8]{1,0:T(4,128)S(1)}, s32[4,8]{1,0:T(4,128)}, u32[]{:S(2)}) copy-start(s32[4,8]{1,0:T(4,128)} %offs_ref.3) | copy-start | bytes 388
  1.4 1.0 %copy-start = (bf16[8,8,4096]{2,1,0:T(8,128)(2,1)S(1)}, bf16[8,8,4096]{2,1,0:T(8,128)(2,1)}, u32[]{:S(2)}) copy-start(bf16[8,8,4096]{2,1,0:T(8,128)(2,1)} %absorb_ref.3) | copy-start | bytes 1572868
  2.4 1.0 %copy-start.1 = (bf16[8,8,4096]{2,1,0:T(8,128)(2,1)S(1)}, bf16[8,8,4096]{2,1,0:T(8,128)(2,1)}, u32[]{:S(2)}) copy-start(bf16[8,8,4096]{2,1,0:T(8,128)(2,1)} %emit_ref.3) | copy-start | bytes 1572868
  3.5 5.1 %copy-start.2 = (f32[8,8,4096]{2,1,0:T(8,128)S(1)}, f32[8,8,4096]{2,1,0:T(8,128)}, u32[]{:S(2)}) copy-start(f32[8,8,4096]{2,1,0:T(8,128)} %measured_ref.1) | copy-start | bytes 3145732
where the time goes:
time: 74.1 us; the launch traced here: 73.8 us
  Pallas kernels  70.3 us (95%)
  local copies, waits for them, and re-layouts  2.84 us (4%)
    pallas_call x1, Pallas kernels, body(): pl.pallas_call(cross_kernel, out_shape=(jax.ShapeDtypeStruct(blocks, f32)...  52.3 us
    pallas_call x1, Pallas kernels, body(): pl.pallas_call(second_kernel, out_shape=(jax.ShapeDtypeStruct(absorb.shap...  12.9 us
    pallas_call x1, Pallas kernels, body(): pl.pallas_call(first_kernel, out_shape=(jax.ShapeDtypeStruct(blocks, f32)...  5.14 us
    unnamed x11, local copies, waits for them, and re-layouts  2.84 us

commit v1 on v0

--- a/solution.py
+++ b/solution.py
@@ -47,7 +47,7 @@
 ):
     slices, rows, columns = absorb_ref.shape
     views = frac_ref.shape[0]
-    count, piece = out_ref.shape[0], out_ref.shape[4]
+    piece = out_ref.shape[4]
     width = 1024
     lower = lax.axis_index("lat") == 0
     for z in range(slices):
@@ -80,8 +80,8 @@
             for i in range(many):
                 dest = ch * (width // piece) + i // per
                 cols = slice((i % per) * lanes, (i % per + 1) * lanes)
-                out_ref[dest, v, 0, :, cols] = run[i]
-                out_ref[dest, v, 1, :, cols] = light[i]
+                out_ref[v, dest, 0, :, cols] = run[i]
+                out_ref[v, dest, 1, :, cols] = light[i]
             return 0
 
         return lax.fori_loop(0, columns // width, chunk_loop, 0)
@@ -90,77 +90,125 @@
 
 
 def cross_kernel(
-    mine_ref, measured_ref, cam_ref, edge_ref, back_ref, rim_ref, got, sent, s1, r1, s2, r2, s3, r3
+    mine_ref, measured_ref, cam_ref, edge_ref, back_ref, rim_ref,
+    other, pair, got, sent, ret, give, sa, ra, sb, rb, sd, rd, sc, rc, s3, r3,
 ):
-    count, views, _, rows, piece = mine_ref.shape
+    views, count, _, rows, piece = mine_ref.shape
     cameras = measured_ref.shape[0]
+    half = count // 2
     me = lax.axis_index("depth")
     lat = lax.axis_index("lat")
+    high, low = me // 2, lax.rem(me, 2)
+    partner = high * 2 + 1 - low
+    near = low == 0
     barrier = pltpu.get_barrier_semaphore()
-    for p in range(1, count):
+
+    def line(p):
+        return lax.rem(high + p, half)
+
+    def send(src, dst, send_sem, recv_sem, to):
+        return pltpu.make_async_remote_copy(
+            src_ref=src, dst_ref=dst, send_sem=send_sem, recv_sem=recv_sem,
+            device_id={"depth": to}, device_id_type=MESH,
+        )
+
+    for p in range(1, half):
         pl.semaphore_signal(
-            barrier, inc=1, device_id={"depth": lax.rem(me + p, count)}, device_id_type=MESH
+            barrier, inc=1, device_id={"depth": line(p) * 2 + low}, device_id_type=MESH
         )
+    pl.semaphore_signal(barrier, inc=1, device_id={"depth": partner}, device_id_type=MESH)
     pl.semaphore_signal(barrier, inc=1, device_id={"lat": 1 - lat}, device_id_type=MESH)
-    pl.semaphore_wait(barrier, count)
-
-    def out_copy(v, p):
-        to = lax.rem(me + p, count)
-        return pltpu.make_async_remote_copy(
-            src_ref=mine_ref.at[to, v],
-            dst_ref=got.at[me, v],
-            send_sem=s1.at[v, p],
-            recv_sem=r1.at[v, p],
-            device_id={"depth": to},
-            device_id_type=MESH,
-        )
-
-    def ret_copy(v, p):
-        to = lax.rem(me + p, count)
-        return pltpu.make_async_remote_copy(
-            src_ref=sent.at[to, v],
-            dst_ref=back_ref.at[me, v],
-            send_sem=s2.at[v, p],
-            recv_sem=r2.at[v, p],
-            device_id={"depth": to},
-            device_id_type=MESH,
-        )
+    pl.semaphore_wait(barrier, half + 1)
+
+    def to_pair(v):
+        src = mine_ref.at[v, pl.ds((1 - low) * half, half)]
+        return send(src, other.at[v], sa.at[v], ra.at[v], partner)
+
+    def to_line(v, p):
+        to = line(p)
+        return send(pair.at[v, to], got.at[v, high], sb.at[v, p], rb.at[v, p], to * 2 + low)
+
+    def from_line(v, p):
+        to = line(p)
+        return send(sent.at[v, to], ret.at[v, high], sd.at[v, p], rd.at[v, p], to * 2 + low)
+
+    def from_pair(v):
+        dst = back_ref.at[v, pl.ds(low * half, half)]
+        return send(give.at[v], dst, sc.at[v], rc.at[v], partner)
 
     for v in range(views):
-        for p in range(1, count):
-            out_copy(v, p).start()
+        to_pair(v).start()
     rim = pltpu.make_async_remote_copy(
         src_ref=edge_ref, dst_ref=rim_ref, send_sem=s3, recv_sem=r3,
         device_id={"lat": 1 - lat}, device_id_type=MESH,
     )
     rim.start()
-    for v in range(views):
-        got[me, v] = mine_ref[me, v]
-    start = pl.multiple_of(me * piece, piece)
-    for v in range(views):
-        for p in range(1, count):
-            out_copy(v, p).wait_recv()
+    start = pl.multiple_of((low * half + high) * piece, piece)
+
+    def combine(v):
+        to_pair(v).wait_recv()
+        for p in [*range(1, half), 0]:
+            h = line(p)
+            own_t, own_l = mine_ref[v, low * half + h, 0], mine_ref[v, low * half + h, 1]
+            oth_t, oth_l = other[v, h, 0], other[v, h, 1]
+            trans = own_t * oth_t
+            light = jnp.where(near, own_l + own_t * oth_l, oth_l + oth_t * own_l)
+            if p:
+                pair[v, h, 0] = trans
+                pair[v, h, 1] = light
+                to_line(v, p).start()
+            else:
+                got[v, h, 0] = trans
+                got[v, h, 1] = light
+
+    def scan(v):
+        for p in range(1, half):
+            to_line(v, p).wait_recv()
         fronts = [jnp.ones((rows, piece), jnp.float32)]
-        for j in range(count):
-            fronts.append(fronts[-1] * got[j, v, 0])
+        for j in range(half - 1):
+            fronts.append(fronts[-1] * got[v, j, 0])
         behind = jnp.zeros((rows, piece), jnp.float32)
-        for j in reversed(range(count)):
-            sent[j, v, 1] = behind
-            behind = got[j, v, 1] + got[j, v, 0] * behind
+        for j in reversed(range(half)):
+            sent[v, j, 1] = behind
+            behind = got[v, j, 1] + got[v, j, 0] * behind
         adjoint = jnp.zeros((rows, piece), jnp.float32)
         for k in range(cameras):
             seen = jnp.where(cam_ref[k, 0] == v, 1.0, 0.0).astype(jnp.float32)
             adjoint += seen * (behind - measured_ref[k, :, pl.ds(start, piece)])
-        for j in range(count):
-            sent[j, v, 0] = adjoint * fronts[j]
-        for p in range(1, count):
-            ret_copy(v, p).start()
-        back_ref[me, v] = sent[me, v]
+        for j in range(half):
+            sent[v, j, 0] = adjoint * fronts[j]
+        for p in range(1, half):
+            from_line(v, p).start()
+        ret[v, high] = sent[v, high]
+
+    def spread(v):
+        for p in range(1, half):
+            from_line(v, p).wait_recv()
+        for h in range(half):
+            at = low * half + h
+            own_t, own_l = mine_ref[v, at, 0], mine_ref[v, at, 1]
+            oth_t, oth_l = other[v, h, 0], other[v, h, 1]
+            front, behind = ret[v, h, 0], ret[v, h, 1]
+            give[v, h, 0] = jnp.where(near, front * own_t, front)
+            give[v, h, 1] = jnp.where(near, behind, own_l + own_t * behind)
+            back_ref[v, at, 0] = jnp.where(near, front, front * oth_t)
+            back_ref[v, at, 1] = jnp.where(near, oth_l + oth_t * behind, behind)
+        from_pair(v).start()
+
+    for turn in range(views + 2):
+        if turn < views:
+            combine(turn)
+        if 0 <= turn - 1 < views:
+            scan(turn - 1)
+        if 0 <= turn - 2 < views:
+            spread(turn - 2)
     rim.wait()
     for v in range(views):
-        for p in range(1, count):
-            out_copy(v, p).wait_send()
-            ret_copy(v, p).wait()
+        to_pair(v).wait_send()
+        for p in range(1, half):
+            to_line(v, p).wait_send()
+            from_line(v, p).wait_send()
+        from_pair(v).wait()
 
 
 def second_kernel(
@@ -169,7 +217,7 @@
 ):
     slices, rows, columns = absorb_ref.shape
     views = frac_ref.shape[0]
-    count, piece = back_ref.shape[0], back_ref.shape[4]
+    piece = back_ref.shape[4]
     width = min(512, columns)
     lower = lax.axis_index("lat") == 0
     for z in range(slices):
@@ -189,11 +237,11 @@
                 if piece >= width:
                     first = ch // (piece // width)
                     inner = pl.multiple_of((ch % (piece // width)) * width, width)
-                    return tiles(back_ref[first, v, q, :, pl.ds(inner, width)])
+                    return tiles(back_ref[v, first, q, :, pl.ds(inner, width)])
                 parts = []
                 for i in range(many):
                     cols = slice((i % per) * lanes, (i % per + 1) * lanes)
-                    parts.append(back_ref[ch * (width // piece) + i // per, v, q, :, cols])
+                    parts.append(back_ref[v, ch * (width // piece) + i // per, q, :, cols])
                 return parts
 
             run = entering(0)
@@ -273,7 +321,9 @@
     scalar = pl.BlockSpec(memory_space=pltpu.SMEM)
     f32 = jnp.float32
     wide = pltpu.VMEM((slices, rows, columns + lanes), f32)
-    blocks = (count, views, 2, rows, piece)
+    blocks = (views, count, 2, rows, piece)
+    half = count // 2
+    part = pltpu.VMEM((views, half, 2, rows, piece), f32)
     sums, edge = pl.pallas_call(
         first_kernel,
         out_shape=(
@@ -296,9 +346,8 @@
         in_specs=[whole, whole, scalar, whole],
         out_specs=(whole, whole),
         scratch_shapes=[
-            pltpu.VMEM(blocks, f32),
-            pltpu.VMEM(blocks, f32),
-            dma((views, count)), dma((views, count)), dma((views, count)), dma((views, count)),
+            *[part] * 6,
+            *[dma((views,))] * 2, *[dma((views, half))] * 4, *[dma((views,))] * 2,
             dma, dma,
         ],
         compiler_params=pltpu.CompilerParams(

time: 74.1 us -> 62.5 us (0.84)
  Pallas kernels: 70.3 us -> 58.7 us
    pallas_call x1, Pallas kernels: 52.3 us -> 40.7 us  [body(): pl.pallas_call(cross_kernel, out_shape=(jax.ShapeDtypeStruct(blocks, f32)...]
where the time goes in v1:
time: 62.5 us; the launch traced here: 62.3 us
  Pallas kernels  58.7 us (94%)
  local copies, waits for them, and re-layouts  2.84 us (5%)
  between operations  0.67 us (1%)
    pallas_call x1, Pallas kernels, body(): pl.pallas_call(cross_kernel, out_shape=(jax.ShapeDtypeStruct(blocks, f32)...  40.7 us
    pallas_call x1, Pallas kernels, body(): pl.pallas_call(second_kernel, out_shape=(jax.ShapeDtypeStruct(absorb.shap...  12.9 us
    pallas_call x1, Pallas kernels, body(): pl.pallas_call(first_kernel, out_shape=(jax.ShapeDtypeStruct(blocks, f32)...  5.13 us
    unnamed x11, local copies, waits for them, and re-layouts  2.84 us

profile of v1, /device:TPU:0, one launch (start us, length us, event | category | flops | bytes accessed | tf_op | source)
XLA Modules:
  0.0 62.3 jit_solution(11779595720361455946)
XLA Ops:
  0.6 0.0 copy-start.4
  0.6 0.0 copy-start.3
  0.7 0.7 %copy.8.cam_ref = s32[8,1]{1,0:T(8,128)S(1)} copy(s32[8,1]{0,1:T(1,128)} %param.9) | data formatting | bytes 64 | tf_op args[3]
  1.4 0.0 copy-done.4
  1.4 0.0 copy-done.3
  1.4 0.0 copy-start
  1.4 1.0 %copy-done = bf16[8,8,4096]{2,1,0:T(8,128)(2,1)S(1)} copy-done((bf16[8,8,4096]{2,1,0:T(8,128)(2,1)S(1)}, bf16[8,8,4096]{2,1,0:T(8,128)(2,1)}, u32[]{:S(2)}) %copy-start) | copy-done | bytes 524312
  2.4 0.0 copy-start.1
  2.4 1.0 %copy-done.1 = bf16[8,8,4096]{2,1,0:T(8,128)(2,1)S(1)} copy-done((bf16[8,8,4096]{2,1,0:T(8,128)(2,1)S(1)}, bf16[8,8,4096]{2,1,0:T(8,128)(2,1)}, u32[]{:S(2)}) %copy-start.1) | copy-done | bytes 524312
  3.5 0.0 copy-start.2
  3.5 5.1 %bricks.1 = (f32[4,8,2,8,512]{4,3,2,1,0:T(8,128)S(1)}, f32[2,8,4096]{2,1,0:T(8,128)S(1)}) custom-call(bf16[8,8,4096]{2,1,0:T(8,128)(2,1)S(1)} %copy-done, bf16[8,8,4096]{2,1,0:T(8,128)(2,1)S(1)} %copy-done.1, s32[4,8]{1,0:T(4,128)S(1)} %copy-done.3, f32[4]{0:T(128)S(1)} %copy-done.4), custom_call_target="tpu_custom_call" | custom-call | tf_op jit(solution)/shard_map/bricks/pallas_call | solution.py:327
  8.6 0.0 copy-done.2
  8.6 40.7 %exchange.1 = (f32[4,8,2,8,512]{4,3,2,1,0:T(8,128)S(1)}, f32[2,8,4096]{2,1,0:T(8,128)S(1)}) custom-call(f32[4,8,2,8,512]{4,3,2,1,0:T(8,128)S(1)} %get-tuple-element.6.mine_ref, f32[8,8,4096]{2,1,0:T(8,128)S(1)} %copy-done.2, s32[8,1]{1,0:T(8,128)S(1)} %copy.8.cam_ref, f32[2,8,4096]{2,1,0:T(8,128)S(1)} %get-tuple-element.7.edge_ref), custom_call_target="tpu_custom_call" | custom-call | tf_op jit(solution)/shard_map/exchange/pallas_call | solution.py:340
  49.4 12.9 %gradients.1 = (f32[8,8,4096]{2,1,0:T(8,128)}, f32[8,8,4096]{2,1,0:T(8,128)}) custom-call(bf16[8,8,4096]{2,1,0:T(8,128)(2,1)S(1)} %copy-done, bf16[8,8,4096]{2,1,0:T(8,128)(2,1)S(1)} %copy-done.1, s32[4,8]{1,0:T(4,128)S(1)} %copy-done.3, f32[4]{0:T(128)S(1)} %copy-done.4, f32[4,8,2,8,512]{4,3,2,1,0:T(8,128)S(1)} %get-tuple-element.8.back_ref, ...), custom_call_target="tpu_custom_call" | custom-call | tf_op jit(solution)/shard_map/gradients/pallas_call | solution.py:359
Async XLA Ops:
  0.6 0.8 %copy-start.4 = (f32[4]{0:T(128)S(1)}, f32[4]{0:T(128)}, u32[]{:S(2)}) copy-start(f32[4]{0:T(128)} %frac_ref.3) | copy-start | bytes 52
  0.6 0.8 %copy-start.3 = (s32[4,8]{1,0:T(4,128)S(1)}, s32[4,8]{1,0:T(4,128)}, u32[]{:S(2)}) copy-start(s32[4,8]{1,0:T(4,128)} %offs_ref.3) | copy-start | bytes 388
  1.4 1.0 %copy-start = (bf16[8,8,4096]{2,1,0:T(8,128)(2,1)S(1)}, bf16[8,8,4096]{2,1,0:T(8,128)(2,1)}, u32[]{:S(2)}) copy-start(bf16[8,8,4096]{2,1,0:T(8,128)(2,1)} %absorb_ref.3) | copy-start | bytes 1572868
  2.4 1.0 %copy-start.1 = (bf16[8,8,4096]{2,1,0:T(8,128)(2,1)S(1)}, bf16[8,8,4096]{2,1,0:T(8,128)(2,1)}, u32[]{:S(2)}) copy-start(bf16[8,8,4096]{2,1,0:T(8,128)(2,1)} %emit_ref.3) | copy-start | bytes 1572868
  3.5 5.1 %copy-start.2 = (f32[8,8,4096]{2,1,0:T(8,128)S(1)}, f32[8,8,4096]{2,1,0:T(8,128)}, u32[]{:S(2)}) copy-start(f32[8,8,4096]{2,1,0:T(8,128)} %measured_ref.1) | copy-start | bytes 3145732

commit v2 on v1

v2 whole, which is shorter than its diff:
```python
import jax
import jax.numpy as jnp
from jax import lax
from jax.experimental import pallas as pl
from jax.experimental.pallas import tpu as pltpu
from jax.sharding import PartitionSpec as P

reg_absorb = 20.0
reg_emit = 0.05
shift_max = 32
lanes = 128
MESH = pl.DeviceIdType.MESH


def tiles(value):
    return [value[:, i * lanes : (i + 1) * lanes] for i in range(value.shape[1] // lanes)]


def advance(parts, amount, lane):
    turned = [pltpu.roll(part, (lanes - amount) & (lanes - 1), axis=1) for part in parts]
    keep = lane < lanes - amount
    return [jnp.where(keep, turned[i], turned[i + 1]) for i in range(len(parts) - 1)]


def fill(field_ref, near_ref, step_ref, z):
    columns = field_ref.shape[2]
    field = field_ref[z].astype(jnp.float32)
    near = pltpu.roll(field, shift_max, axis=1)
    step = pltpu.roll(field, shift_max - 1, axis=1) - near
    near_ref[z, :, :columns] = near
    near_ref[z, :, columns:] = near[:, :lanes]
    step_ref[z, :, :columns] = step
    step_ref[z, :, columns:] = step[:, :lanes]


def sheared(near_ref, step_ref, z, start, width, amount, weight, lane):
    near = near_ref[z, :, pl.ds(start, width + lanes)]
    step = step_ref[z, :, pl.ds(start, width + lanes)]
    return advance(tiles(near + weight * step), amount, lane)


def fused_kernel(
    absorb_ref, emit_ref, measured_ref, cam_ref, offs_ref, frac_ref, ga_ref, ge_ref,
    near_a, step_a, near_e, step_e, seen_ref, edge_ref, rim_ref, mine_ref, back_ref,
    other, pair, got, sent, ret, give, keep, grad_a, grad_e, sum_a, sum_e,
    sa, ra, sb, rb, sd, rd, sc, rc, s3, r3, sm,
):
    slices, rows, columns = absorb_ref.shape
    views, count, _, _, piece = mine_ref.shape
    cameras = measured_ref.shape[0]
    half = count // 2
    me = lax.axis_index("depth")
    lat = lax.axis_index("lat")
    high, low = me // 2, lax.rem(me, 2)
    partner = high * 2 + 1 - low
    near = low == 0
    barrier = pltpu.get_barrier_semaphore()

    def line(p):
        return lax.rem(high + p, half)

    def send(src, dst, send_sem, recv_sem, to):
        return pltpu.make_async_remote_copy(
            src_ref=src, dst_ref=dst, send_sem=send_sem, recv_sem=recv_sem,
            device_id={"depth": to}, device_id_type=MESH,
        )

    for p in range(1, half):
        pl.semaphore_signal(
            barrier, inc=1, device_id={"depth": line(p) * 2 + low}, device_id_type=MESH
        )
    pl.semaphore_signal(barrier, inc=1, device_id={"depth": partner}, device_id_type=MESH)
    pl.semaphore_signal(barrier, inc=1, device_id={"lat": 1 - lat}, device_id_type=MESH)
    def to_pair(v):
        src = mine_ref.at[v, pl.ds((1 - low) * half, half)]
        return send(src, other.at[v], sa.at[v], ra.at[v], partner)

    def to_line(v, p):
        to = line(p)
        return send(pair.at[v, to], got.at[v, high], sb.at[v, p], rb.at[v, p], to * 2 + low)

    def from_line(v, p):
        to = line(p)
        return send(sent.at[v, to], ret.at[v, high], sd.at[v, p], rd.at[v, p], to * 2 + low)

    def from_pair(v):
        dst = back_ref.at[v, pl.ds(low * half, half)]
        return send(give.at[v], dst, sc.at[v], rc.at[v], partner)

    start = pl.multiple_of((low * half + high) * piece, piece)
    images = pltpu.make_async_copy(measured_ref.at[:, :, pl.ds(start, piece)], seen_ref, sm)
    images.start()
    lower = lat == 0
    for z in range(slices):
        fill(absorb_ref, near_a, step_a, z)
        fill(emit_ref, near_e, step_e, z)
        for f, ref in enumerate((absorb_ref, emit_ref)):
            field = ref[z].astype(jnp.float32)
            edge_ref[f, z : z + 1, :] = jnp.where(lower, field[rows - 1 :], field[:1])
    pl.semaphore_wait(barrier, half + 1)
    rim = pltpu.make_async_remote_copy(
        src_ref=edge_ref, dst_ref=rim_ref, send_sem=s3, recv_sem=r3,
        device_id={"lat": 1 - lat}, device_id_type=MESH,
    )
    rim.start()

    def combine(v):
        to_pair(v).wait_recv()
        for p in [*range(1, half), 0]:
            h = line(p)
            own_t, own_l = mine_ref[v, low * half + h, 0], mine_ref[v, low * half + h, 1]
            oth_t, oth_l = other[v, h, 0], other[v, h, 1]
            trans = own_t * oth_t
            light = jnp.where(near, own_l + own_t * oth_l, oth_l + oth_t * own_l)
            if p:
                pair[v, h, 0] = trans
                pair[v, h, 1] = light
                to_line(v, p).start()
            else:
                got[v, h, 0] = trans
                got[v, h, 1] = light

    def scan(v):
        for p in range(1, half):
            to_line(v, p).wait_recv()
        fronts = [jnp.ones((rows, piece), jnp.float32)]
        for j in range(half - 1):
            fronts.append(fronts[-1] * got[v, j, 0])
        behind = jnp.zeros((rows, piece), jnp.float32)
        for j in reversed(range(half)):
            sent[v, j, 1] = behind
            behind = got[v, j, 1] + got[v, j, 0] * behind
        adjoint = jnp.zeros((rows, piece), jnp.float32)
        for k in range(cameras):
            seen = jnp.where(cam_ref[k : k + 1, :] == v, 1.0, 0.0).astype(jnp.float32)
            adjoint += seen * (behind - seen_ref[k])
        for j in range(half):
            sent[v, j, 0] = adjoint * fronts[j]
        for p in range(1, half):
            from_line(v, p).start()
        ret[v, high] = sent[v, high]

    def spread(v):
        for p in range(1, half):
            from_line(v, p).wait_recv()
        for h in range(half):
            at = low * half + h
            own_t, own_l = mine_ref[v, at, 0], mine_ref[v, at, 1]
            oth_t, oth_l = other[v, h, 0], other[v, h, 1]
            front, behind = ret[v, h, 0], ret[v, h, 1]
            give[v, h, 0] = jnp.where(near, front * own_t, front)
            give[v, h, 1] = jnp.where(near, behind, own_l + own_t * behind)
            back_ref[v, at, 0] = jnp.where(near, front, front * oth_t)
            back_ref[v, at, 1] = jnp.where(near, oth_l + oth_t * behind, behind)
        from_pair(v).start()

    lane = lax.broadcasted_iota(jnp.int32, (rows, lanes), 1)
    per = piece // lanes
    wide = 1024

    def forward(v):
        weight = frac_ref[v]

        def chunk_loop(ch, _):
            begin = pl.multiple_of(ch * wide, wide)
            run, light = None, None
            for z in range(slices):
                amount = offs_ref[v, z] + shift_max
                optical = sheared(near_a, step_a, z, begin, wide, amount, weight, lane)
                glowing = sheared(near_e, step_e, z, begin, wide, amount, weight, lane)
                trans = [jnp.exp(-o) for o in optical]
                radiance = [g * (1.0 - t) for g, t in zip(glowing, trans)]
                at = pl.ds(begin, wide)
                keep[v, z, 0, :, at] = jnp.concatenate(trans, axis=1)
                keep[v, z, 1, :, at] = jnp.concatenate(glowing, axis=1)
                if z == 0:
                    run, light = trans, radiance
                else:
                    keep[v, z, 2, :, at] = jnp.concatenate(run, axis=1)
                    light = [l + r * x for l, r, x in zip(light, run, radiance)]
                    run = [r * t for r, t in zip(run, trans)]
            for i in range(wide // lanes):
                dest = ch * (wide // piece) + i // per
                cols = slice((i % per) * lanes, (i % per + 1) * lanes)
                mine_ref[v, dest, 0, :, cols] = run[i]
                mine_ref[v, dest, 1, :, cols] = light[i]
            return 0

        lax.fori_loop(0, columns // wide, chunk_loop, 0)
        to_pair(v).start()

    def gradient(v, side):
        def piece_loop(h, _):
            p = side * half + h
            at = pl.ds(pl.multiple_of(p * piece, piece), piece)
            front, behind = back_ref[v, p, 0], back_ref[v, p, 1]
            for z in reversed(range(slices)):
                trans, glow = keep[v, z, 0, :, at], keep[v, z, 1, :, at]
                before = front * keep[v, z, 2, :, at] if z else front
                opaque = 1.0 - trans
                grad_e[z, :, at] = before * opaque
                grad_a[z, :, at] = before * trans * (glow - behind)
                behind = glow * opaque + trans * behind
            return 0

        lax.fori_loop(0, half, piece_loop, 0)

    def finish(v):
        from_pair(v).wait_recv()
        gradient(v, 1 - low)
        weight = frac_ref[v]
        for grad in (grad_a, grad_e):
            for z in range(slices):
                grad[z, :, columns:] = grad[z, :, :lanes]

        def slice_loop(z, _):
            amount = shift_max - offs_ref[v, z]
            for grad, total, out in ((grad_a, sum_a, ga_ref), (grad_e, sum_e, ge_ref)):
                near, far = [], []
                for ch in range(columns // wide):
                    parts = tiles(grad[z, :, ch * wide : (ch + 1) * wide + lanes])
                    moved = jnp.concatenate(advance(parts, amount, lane), axis=1)
                    at = slice(ch * wide, (ch + 1) * wide)
                    a, b = (1.0 - weight) * moved, weight * moved
                    if v:
                        a, b = a + total[0, z, :, at], b + total[1, z, :, at]
                    if v < views - 1:
                        total[0, z, :, at] = a
                        total[1, z, :, at] = b
                    near.append(a)
                    far.append(b)
                if v == views - 1:
                    far = pltpu.roll(jnp.concatenate(far, axis=1), 1, axis=1)
                    both = jnp.concatenate(near, axis=1) + far
                    out[z] = out[z] + pltpu.roll(both, shift_max, axis=1)
            return 0

        lax.fori_loop(0, slices, slice_loop, 0)

    def smooth(f, field_ref, out, reg):
        row = lax.broadcasted_iota(jnp.int32, (rows, columns), 0)
        col = lax.broadcasted_iota(jnp.int32, (rows, columns), 1)
        for z in range(slices):
            field = field_ref[z].astype(jnp.float32)
            edge = rim_ref[f, z : z + 1, :]
            up = jnp.where(row == 0, jnp.where(lower, 0.0, edge), pltpu.roll(field, 1, axis=0))
            down = jnp.where(
                row == rows - 1, jnp.where(lower, edge, 0.0), pltpu.roll(field, rows - 1, axis=0)
            )
            left = jnp.where(col == 0, 0.0, pltpu.roll(field, 1, axis=1))
            right = jnp.where(col == columns - 1, 0.0, pltpu.roll(field, columns - 1, axis=1))
            out[z] = -reg * (down + up + right + left - 4.0 * field)

    for v in range(views - 1):
        forward(v)
    images.wait()
    for turn in range(views + 3):
        if turn < views:
            combine(turn)
        if turn == 0:
            forward(views - 1)
        if 0 <= turn - 1 < views:
            scan(turn - 1)
        if turn == 1:
            rim.wait_recv()
            smooth(0, absorb_ref, ga_ref, reg_absorb)
            smooth(1, emit_ref, ge_ref, reg_emit)
        if 0 <= turn - 2 < views:
            spread(turn - 2)
        if 0 <= turn - 3 < views:
            finish(turn - 3)
        if 0 <= turn - 2 < views:
            gradient(turn - 2, low)
    rim.wait_send()
    for v in range(views):
        to_pair(v).wait_send()
        for p in range(1, half):
            to_line(v, p).wait_send()
            from_line(v, p).wait_send()
        from_pair(v).wait_send()


def body(absorb, emission, measured, camera_view, offsets, fractions):
    slices, rows, columns = absorb.shape
    views, cameras = offsets.shape[0], measured.shape[0]
    count = lax.axis_size("depth")
    half, piece = count // 2, columns // count
    whole = pl.BlockSpec(memory_space=pltpu.VMEM)
    scalar = pl.BlockSpec(memory_space=pltpu.SMEM)
    dma = pltpu.SemaphoreType.DMA

    def room(*shape):
        return pltpu.VMEM(shape, jnp.float32)

    padded = room(slices, rows, columns + lanes)
    return pl.pallas_call(
        fused_kernel,
        out_shape=(
            jax.ShapeDtypeStruct(absorb.shape, jnp.float32),
            jax.ShapeDtypeStruct(absorb.shape, jnp.float32),
        ),
        in_specs=[whole, whole, pl.BlockSpec(memory_space=pl.ANY), whole, scalar, scalar],
        out_specs=(whole, whole),
        scratch_shapes=[
            *[padded] * 4,
            room(cameras, rows, piece),
            *[room(2, slices, columns)] * 2,
            *[room(views, count, 2, rows, piece)] * 2,
            *[room(views, half, 2, rows, piece)] * 6,
            room(views, slices, 3, rows, columns),
            *[padded] * 2,
            *[room(2, slices, rows, columns)] * 2,
            *[dma((views,))] * 2, *[dma((views, half))] * 4, *[dma((views,))] * 2,
            dma, dma, dma,
        ],
        compiler_params=pltpu.CompilerParams(
            vmem_limit_bytes=52 * 1024 * 1024, collective_id=0, has_side_effects=True
        ),
        name="tomography",
    )(absorb, emission, measured, camera_view, offsets, fractions)


def solution(mesh):
    placed = (
        P("depth", ("groups", "lat"), None),
        P("depth", ("groups", "lat"), None),
        P(None, ("groups", "lat"), None),
        P(),
        P(None, "depth"),
        P(),
    )
    return jax.shard_map(
        body,
        mesh=mesh,
        in_specs=placed,
        out_specs=(P("depth", ("groups", "lat"), None), P("depth", ("groups", "lat"), None)),
        check_vma=False,
    )
```

time: 62.5 us -> 53.5 us (0.86)
  Pallas kernels: 58.7 us -> 46.4 us
  local copies, waits for them, and re-layouts: 2.84 us -> 6.17 us
    pallas_call x3 -> x1, Pallas kernels: 58.7 us -> 46.4 us  [body(): pl.pallas_call(fused_kernel, out_shape=(jax.ShapeDtypeStruct(absorb.shape...]
    unnamed x11 -> x13, local copies, waits for them, and re-layouts: 2.84 us -> 6.17 us
where the time goes in v2:
time: 53.5 us; the launch traced here: 53.3 us
  Pallas kernels  46.4 us (87%)
  local copies, waits for them, and re-layouts  6.17 us (12%)
  between operations  0.67 us (1%)
    pallas_call x1, Pallas kernels, body(): pl.pallas_call(fused_kernel, out_shape=(jax.ShapeDtypeStruct(absorb.shape...  46.4 us
    unnamed x13, local copies, waits for them, and re-layouts  6.17 us

profile of v2, /device:TPU:0, one launch (start us, length us, event | category | flops | bytes accessed | tf_op | source)
XLA Modules:
  0.0 53.3 jit_solution(17119301418668757243)
XLA Ops:
  0.6 0.0 copy-start.3
  0.6 0.0 copy-start.2
  0.7 0.7 %copy.8.cam_ref = s32[8,1]{1,0:T(8,128)S(1)} copy(s32[8,1]{0,1:T(1,128)} %param.9) | data formatting | bytes 64 | tf_op args[3]
  1.4 0.0 copy-done.3
  1.4 0.0 copy-done.2
  1.4 0.0 copy-start
  1.4 1.0 %copy-done = bf16[8,8,4096]{2,1,0:T(8,128)(2,1)S(1)} copy-done((bf16[8,8,4096]{2,1,0:T(8,128)(2,1)S(1)}, bf16[8,8,4096]{2,1,0:T(8,128)(2,1)}, u32[]{:S(2)}) %copy-start) | copy-done | bytes 524312
  2.4 0.0 copy-start.1
  2.4 1.0 %copy-done.1 = bf16[8,8,4096]{2,1,0:T(8,128)(2,1)S(1)} copy-done((bf16[8,8,4096]{2,1,0:T(8,128)(2,1)S(1)}, bf16[8,8,4096]{2,1,0:T(8,128)(2,1)}, u32[]{:S(2)}) %copy-start.1) | copy-done | bytes 524312
  3.5 46.4 %tomography.1 = (f32[8,8,4096]{2,1,0:T(8,128)}, f32[8,8,4096]{2,1,0:T(8,128)}) custom-call(bf16[8,8,4096]{2,1,0:T(8,128)(2,1)S(1)} %copy-done, bf16[8,8,4096]{2,1,0:T(8,128)(2,1)S(1)} %copy-done.1, f32[8,8,4096]{2,1,0:T(8,128)} %measured_ref.1, s32[8,1]{1,0:T(8,128)S(1)} %copy.8.cam_ref, s32[4,8]{1,0:T(4,128)S(1)} %copy-done.2, f32[4]{0:T(128)S(1)} %copy-done.3), custom_call_target="tpu_custom_call" | custom-call | tf_op jit(solution)/shard_map/tomography/pallas_call | solution.py:296
  49.9 0.0 copy-start.4
  49.9 2.4 %copy.11 = f32[8,8,4096]{2,1,0:T(8,128)} copy(f32[8,8,4096]{2,1,0:T(8,128)} %get-tuple-element.4) | data formatting | bytes 2097152
  52.3 0.0 copy-done.4
  52.3 1.0 %copy.12 = f32[8,8,4096]{2,1,0:T(8,128)} copy(f32[8,8,4096]{2,1,0:T(8,128)S(1)} %copy-done.4) | data formatting | bytes 2097152
Async XLA Ops:
  0.6 0.8 %copy-start.3 = (f32[4]{0:T(128)S(1)}, f32[4]{0:T(128)}, u32[]{:S(2)}) copy-start(f32[4]{0:T(128)} %frac_ref.1) | copy-start | bytes 52
  0.6 0.8 %copy-start.2 = (s32[4,8]{1,0:T(4,128)S(1)}, s32[4,8]{1,0:T(4,128)}, u32[]{:S(2)}) copy-start(s32[4,8]{1,0:T(4,128)} %offs_ref.1) | copy-start | bytes 388
  1.4 1.0 %copy-start = (bf16[8,8,4096]{2,1,0:T(8,128)(2,1)S(1)}, bf16[8,8,4096]{2,1,0:T(8,128)(2,1)}, u32[]{:S(2)}) copy-start(bf16[8,8,4096]{2,1,0:T(8,128)(2,1)} %absorb_ref.1) | copy-start | bytes 1572868
  2.4 1.0 %copy-start.1 = (bf16[8,8,4096]{2,1,0:T(8,128)(2,1)S(1)}, bf16[8,8,4096]{2,1,0:T(8,128)(2,1)}, u32[]{:S(2)}) copy-start(bf16[8,8,4096]{2,1,0:T(8,128)(2,1)} %emit_ref.1) | copy-start | bytes 1572868
  49.9 2.4 %copy-start.4 = (f32[8,8,4096]{2,1,0:T(8,128)S(1)}, f32[8,8,4096]{2,1,0:T(8,128)}, u32[]{:S(2)}) copy-start(f32[8,8,4096]{2,1,0:T(8,128)} %get-tuple-element.5) | copy-start | bytes 3145732

commit v3 on v2

--- a/solution.py
+++ b/solution.py
@@ -40,13 +40,20 @@
 
 
 def fused_kernel(
-    absorb_ref, emit_ref, measured_ref, cam_ref, offs_ref, frac_ref, ga_ref, ge_ref,
+    absorb_hbm, emit_hbm, measured_ref, cam_ref, offs_ref, frac_ref, ga_ref, ge_ref,
+    absorb_ref, emit_ref,
     near_a, step_a, near_e, step_e, seen_ref, edge_ref, rim_ref, mine_ref, back_ref,
     other, pair, got, sent, ret, give, keep, grad_a, grad_e, sum_a, sum_e,
-    sa, ra, sb, rb, sd, rd, sc, rc, s3, r3, sm,
+    sa, ra, sb, rb, sd, rd, sc, rc, s3, r3, sm, si,
 ):
     slices, rows, columns = absorb_ref.shape
     views, count, _, _, piece = mine_ref.shape
+    loads = [
+        pltpu.make_async_copy(src, dst, si.at[i])
+        for i, (src, dst) in enumerate(((absorb_hbm, absorb_ref), (emit_hbm, emit_ref)))
+    ]
+    for load in loads:
+        load.start()
     cameras = measured_ref.shape[0]
     half = count // 2
     me = lax.axis_index("depth")
@@ -91,6 +98,8 @@
     images = pltpu.make_async_copy(measured_ref.at[:, :, pl.ds(start, piece)], seen_ref, sm)
     images.start()
     lower = lat == 0
+    for load in loads:
+        load.wait()
     for z in range(slices):
         fill(absorb_ref, near_a, step_a, z)
         fill(emit_ref, near_e, step_e, z)
@@ -106,6 +115,8 @@
 
     def combine(v):
         to_pair(v).wait_recv()
+        if v + ahead < views - 1:
+            to_pair(v + ahead).start()
         for p in [*range(1, half), 0]:
             h = line(p)
             own_t, own_l = mine_ref[v, low * half + h, 0], mine_ref[v, low * half + h, 1]
@@ -132,7 +143,7 @@
             behind = got[v, j, 1] + got[v, j, 0] * behind
         adjoint = jnp.zeros((rows, piece), jnp.float32)
         for k in range(cameras):
-            seen = jnp.where(cam_ref[k : k + 1, :] == v, 1.0, 0.0).astype(jnp.float32)
+            seen = jnp.where(cam_ref[0, k] == v, 1.0, 0.0).astype(jnp.float32)
             adjoint += seen * (behind - seen_ref[k])
         for j in range(half):
             sent[v, j, 0] = adjoint * fronts[j]
@@ -187,7 +198,6 @@
             return 0
 
         lax.fori_loop(0, columns // wide, chunk_loop, 0)
-        to_pair(v).start()
 
     def gradient(v, side):
         def piece_loop(h, _):
@@ -251,26 +261,32 @@
             right = jnp.where(col == columns - 1, 0.0, pltpu.roll(field, columns - 1, axis=1))
             out[z] = -reg * (down + up + right + left - 4.0 * field)
 
+    ahead = 2
     for v in range(views - 1):
         forward(v)
+        if v < ahead:
+            to_pair(v).start()
     images.wait()
     for turn in range(views + 3):
         if turn < views:
             combine(turn)
         if turn == 0:
             forward(views - 1)
+        if turn == views - 1 - ahead:
+            to_pair(views - 1).start()
         if 0 <= turn - 1 < views:
             scan(turn - 1)
         if turn == 1:
             rim.wait_recv()
             smooth(0, absorb_ref, ga_ref, reg_absorb)
-            smooth(1, emit_ref, ge_ref, reg_emit)
         if 0 <= turn - 2 < views:
             spread(turn - 2)
         if 0 <= turn - 3 < views:
             finish(turn - 3)
         if 0 <= turn - 2 < views:
             gradient(turn - 2, low)
+        if turn == 2:
+            smooth(1, emit_ref, ge_ref, reg_emit)
     rim.wait_send()
     for v in range(views):
         to_pair(v).wait_send()
@@ -286,6 +302,7 @@
     count = lax.axis_size("depth")
     half, piece = count // 2, columns // count
     whole = pl.BlockSpec(memory_space=pltpu.VMEM)
+    hbm = pl.BlockSpec(memory_space=pltpu.HBM)
     scalar = pl.BlockSpec(memory_space=pltpu.SMEM)
     dma = pltpu.SemaphoreType.DMA
 
@@ -299,9 +316,10 @@
             jax.ShapeDtypeStruct(absorb.shape, jnp.float32),
             jax.ShapeDtypeStruct(absorb.shape, jnp.float32),
         ),
-        in_specs=[whole, whole, pl.BlockSpec(memory_space=pl.ANY), whole, scalar, scalar],
+        in_specs=[hbm, hbm, hbm, scalar, scalar, scalar],
         out_specs=(whole, whole),
         scratch_shapes=[
+            *[pltpu.VMEM(absorb.shape, absorb.dtype)] * 2,
             *[padded] * 4,
             room(cameras, rows, piece),
             *[room(2, slices, columns)] * 2,
@@ -311,13 +329,13 @@
             *[padded] * 2,
             *[room(2, slices, rows, columns)] * 2,
             *[dma((views,))] * 2, *[dma((views, half))] * 4, *[dma((views,))] * 2,
-            dma, dma, dma,
+            dma, dma, dma, dma((2,)),
         ],
         compiler_params=pltpu.CompilerParams(
-            vmem_limit_bytes=52 * 1024 * 1024, collective_id=0, has_side_effects=True
+            vmem_limit_bytes=60 * 1024 * 1024, collective_id=0, has_side_effects=True
         ),
         name="tomography",
-    )(absorb, emission, measured, camera_view, offsets, fractions)
+    )(absorb, emission, measured, camera_view.T, offsets, fractions)
 
 
 def solution(mesh):

time: 53.5 us -> 50.7 us (0.948)
  local copies, waits for them, and re-layouts: 6.17 us -> 3.33 us
    unnamed x13 -> x4, local copies, waits for them, and re-layouts: 6.17 us -> 3.33 us
where the time goes in v3:
time: 50.7 us; the launch traced here: 50.5 us
  Pallas kernels  46.5 us (92%)
  local copies, waits for them, and re-layouts  3.33 us (7%)
  between operations  0.65 us (1%)
    pallas_call x1, Pallas kernels, body(): pl.pallas_call(fused_kernel, out_shape=(jax.ShapeDtypeStruct(absorb.shape...  46.5 us
    unnamed x4, local copies, waits for them, and re-layouts  3.33 us

profile of v3, /device:TPU:0, one launch (start us, length us, event | category | flops | bytes accessed | tf_op | source)
XLA Modules:
  0.0 50.5 jit_solution(17817008620973678710)
XLA Ops:
  0.6 46.5 %tomography.1 = (f32[8,8,4096]{2,1,0:T(8,128)}, f32[8,8,4096]{2,1,0:T(8,128)}) custom-call(bf16[8,8,4096]{2,1,0:T(8,128)(2,1)} %absorb_hbm.1, bf16[8,8,4096]{2,1,0:T(8,128)(2,1)} %emit_hbm.1, f32[8,8,4096]{2,1,0:T(8,128)} %measured_ref.1, s32[1,8]{1,0:T(1,128)} %bitcast.1, s32[4,8]{1,0:T(4,128)} %offs_ref.1, f32[4]{0:T(128)} %frac_ref.1), custom_call_target="tpu_custom_call" | custom-call | tf_op jit(solution)/shard_map/tomography/pallas_call | solution.py:313
  47.1 0.0 copy-start
  47.2 2.4 %copy.10 = f32[8,8,4096]{2,1,0:T(8,128)} copy(f32[8,8,4096]{2,1,0:T(8,128)} %get-tuple-element.4) | data formatting | bytes 2097152
  49.5 0.0 copy-done
  49.5 1.0 %copy.11 = f32[8,8,4096]{2,1,0:T(8,128)} copy(f32[8,8,4096]{2,1,0:T(8,128)S(1)} %copy-done) | data formatting | bytes 2097152
Async XLA Ops:
  47.1 2.4 %copy-start = (f32[8,8,4096]{2,1,0:T(8,128)S(1)}, f32[8,8,4096]{2,1,0:T(8,128)}, u32[]{:S(2)}) copy-start(f32[8,8,4096]{2,1,0:T(8,128)} %get-tuple-element.5) | copy-start | bytes 3145732

commit v4 on v3

--- a/solution.py
+++ b/solution.py
@@ -40,11 +40,11 @@
 
 
 def fused_kernel(
-    absorb_hbm, emit_hbm, measured_ref, cam_ref, offs_ref, frac_ref, ga_ref, ge_ref,
-    absorb_ref, emit_ref,
+    absorb_hbm, emit_hbm, measured_ref, cam_ref, offs_ref, frac_ref, ga_hbm, ge_hbm,
+    ga_ref, ge_ref, absorb_ref, emit_ref,
     near_a, step_a, near_e, step_e, seen_ref, edge_ref, rim_ref, mine_ref, back_ref,
     other, pair, got, sent, ret, give, keep, grad_a, grad_e, sum_a, sum_e,
-    sa, ra, sb, rb, sd, rd, sc, rc, s3, r3, sm, si,
+    sa, ra, sb, rb, sd, rd, sc, rc, s3, r3, sm, si, so,
 ):
     slices, rows, columns = absorb_ref.shape
     views, count, _, _, piece = mine_ref.shape
@@ -215,6 +215,10 @@
 
         lax.fori_loop(0, half, piece_loop, 0)
 
+    def store(out, z):
+        f, dst = (0, ga_hbm) if out is ga_ref else (1, ge_hbm)
+        return pltpu.make_async_copy(out.at[z], dst.at[z], so.at[f, z])
+
     def finish(v):
         from_pair(v).wait_recv()
         gradient(v, 1 - low)
@@ -243,6 +247,7 @@
                     far = pltpu.roll(jnp.concatenate(far, axis=1), 1, axis=1)
                     both = jnp.concatenate(near, axis=1) + far
                     out[z] = out[z] + pltpu.roll(both, shift_max, axis=1)
+                    store(out, z).start()
             return 0
 
         lax.fori_loop(0, slices, slice_loop, 0)
@@ -287,6 +292,9 @@
             gradient(turn - 2, low)
         if turn == 2:
             smooth(1, emit_ref, ge_ref, reg_emit)
+    for z in range(slices):
+        store(ga_ref, z).wait()
+        store(ge_ref, z).wait()
     rim.wait_send()
     for v in range(views):
         to_pair(v).wait_send()
@@ -301,7 +309,6 @@
     views, cameras = offsets.shape[0], measured.shape[0]
     count = lax.axis_size("depth")
     half, piece = count // 2, columns // count
-    whole = pl.BlockSpec(memory_space=pltpu.VMEM)
     hbm = pl.BlockSpec(memory_space=pltpu.HBM)
     scalar = pl.BlockSpec(memory_space=pltpu.SMEM)
     dma = pltpu.SemaphoreType.DMA
@@ -317,8 +324,9 @@
             jax.ShapeDtypeStruct(absorb.shape, jnp.float32),
         ),
         in_specs=[hbm, hbm, hbm, scalar, scalar, scalar],
-        out_specs=(whole, whole),
+        out_specs=(hbm, hbm),
         scratch_shapes=[
+            *[room(slices, rows, columns)] * 2,
             *[pltpu.VMEM(absorb.shape, absorb.dtype)] * 2,
             *[padded] * 4,
             room(cameras, rows, piece),
@@ -329,7 +337,7 @@
             *[padded] * 2,
             *[room(2, slices, rows, columns)] * 2,
             *[dma((views,))] * 2, *[dma((views, half))] * 4, *[dma((views,))] * 2,
-            dma, dma, dma, dma((2,)),
+            dma, dma, dma, dma((2,)), dma((2, slices)),
         ],
         compiler_params=pltpu.CompilerParams(
             vmem_limit_bytes=60 * 1024 * 1024, collective_id=0, has_side_effects=True

time: 50.7 us -> 50.1 us (0.988)
  Pallas kernels: 46.5 us -> 45.9 us
    pallas_call x1, Pallas kernels: 46.5 us -> 45.9 us  [body(): pl.pallas_call(fused_kernel, out_shape=(jax.ShapeDtypeStruct(absorb.shape...]
where the time goes in v4:
time: 50.1 us; the launch traced here: 49.9 us
  Pallas kernels  45.9 us (92%)
  local copies, waits for them, and re-layouts  3.33 us (7%)
  between operations  0.65 us (1%)
    pallas_call x1, Pallas kernels, body(): pl.pallas_call(fused_kernel, out_shape=(jax.ShapeDtypeStruct(absorb.shape...  45.9 us
    unnamed x4, local copies, waits for them, and re-layouts  3.33 us

profile of v4, /device:TPU:0, one launch (start us, length us, event | category | flops | bytes accessed | tf_op | source)
XLA Modules:
  0.0 49.9 jit_solution(15827309030582984797)
XLA Ops:
  0.6 45.9 %tomography.1 = (f32[8,8,4096]{2,1,0:T(8,128)}, f32[8,8,4096]{2,1,0:T(8,128)}) custom-call(bf16[8,8,4096]{2,1,0:T(8,128)(2,1)} %absorb_hbm.1, bf16[8,8,4096]{2,1,0:T(8,128)(2,1)} %emit_hbm.1, f32[8,8,4096]{2,1,0:T(8,128)} %measured_ref.1, s32[1,8]{1,0:T(1,128)} %bitcast.1, s32[4,8]{1,0:T(4,128)} %offs_ref.1, f32[4]{0:T(128)} %frac_ref.1), custom_call_target="tpu_custom_call" | custom-call | tf_op jit(solution)/shard_map/tomography/pallas_call | solution.py:320
  46.6 0.0 copy-start
  46.6 2.4 %copy.10 = f32[8,8,4096]{2,1,0:T(8,128)} copy(f32[8,8,4096]{2,1,0:T(8,128)} %get-tuple-element.4) | data formatting | bytes 2097152
  49.0 0.0 copy-done
  49.0 1.0 %copy.11 = f32[8,8,4096]{2,1,0:T(8,128)} copy(f32[8,8,4096]{2,1,0:T(8,128)S(1)} %copy-done) | data formatting | bytes 2097152
Async XLA Ops:
  46.6 2.4 %copy-start = (f32[8,8,4096]{2,1,0:T(8,128)S(1)}, f32[8,8,4096]{2,1,0:T(8,128)}, u32[]{:S(2)}) copy-start(f32[8,8,4096]{2,1,0:T(8,128)} %get-tuple-element.5) | copy-start | bytes 3145732
